TPU v7x, 256 devices: a whole 4x4x8 slice. The times are simulated.
256 devices in a mesh: gx: 32 (over z_lo, y, core), gy: 8 (over x, z_hi).
Axes of the slice: x: 4, y: 4, z: 8 (z_hi: 2, z_lo: 4; z = z_hi * 4 + z_lo), core: 2. Of those that a mesh axis runs over, the one named last changes fastest.
Arguments:
- features: bfloat16 [512, 512, 128], P(('gx', 'gy')), may hold values from -6 to 6
- occupied: int32 [512, 512], P(('gx', 'gy')), may hold values 0 or 1
- weight_one: bfloat16 [27, 128, 128], replicated, may hold values from -0.109375 to 0.109375
- bias_one: float32 [128], replicated, may hold values from -3 to 3
- weight_two: bfloat16 [27, 128, 128], replicated, may hold values from -0.109375 to 0.109375
- cotangent: bfloat16 [512, 512, 128], P(('gx', 'gy')), may hold values from -6 to 6
- neighbours: int32 [512, 27], P(('gx', 'gy')), may hold values from 0 to 18, as said below
- send_x: int32 [256, 2, 6], P(('gx', 'gy')), may hold values from 0 to 18, as said below
- send_y: int32 [256, 2, 2], P(('gx', 'gy')), may hold values from 0 to 18, as said below
Outputs:
- output: bfloat16 [512, 512, 128], P(('gx', 'gy'))
- grad_features: bfloat16 [512, 512, 128], P(('gx', 'gy'))
- grad_weight_one: float32 [27, 128, 128], replicated
- grad_weight_two: float32 [27, 128, 128], replicated
Inputs may be any that keep to these rules, and one draw needn't show every extreme that they name: `neighbours`: each tile is 2 x 2 x 2 bricks of the map, tiles laid out with x over gx and y over gy. A tile's live bricks fill its first slots, and some tile is full in every draw. A live brick's entry k names the pool row holding the brick at brick offset (k // 9 - 1, k // 3 % 3 - 1, k % 3 - 1), or 18 where that brick is empty or lies outside the map; entry 13 names its own slot; a dead slot's entries are all 18. The lists describe one map, so neighbourhood is symmetric. send_y[t, 0] lists in slot order the live slots of tile t in its top layer of bricks along y, send_y[t, 1] those in its bottom layer; the rest is 18. send_x[t, 0] lists in row order the pool rows below 6 of tile t (its own bricks and those it received along y) whose bricks lie in its top layer along x, send_x[t, 1] those in its bottom layer; the rest is 18.
All inputs are finite; a program needn't handle non-finite values. No bound on the sum of `occupied` on one device may be relied on, other than what follows from the above.
Results may differ from a plain program's by a relative error of at most 0.015.
Values may be sent and summed in bfloat16 or wider, within the bound.
A program may use at most 128 MiB of HBM per device.

v0:
```python
import math
import jax
import jax.numpy as jnp
from jax import lax
from jax.sharding import PartitionSpec as P

EDGE = 8
KVOL = 27


def shifted(block, axis, distance):
    devices = range(lax.axis_size(axis))
    route = [(i - distance, i) for i in devices if i - distance in devices]
    return lax.ppermute(block, axis, route)


def cut_layer(portion, side_code, along_axis):
    extent = portion.shape[along_axis]
    if side_code == 0:
        return lax.slice_in_dim(portion, extent - 1, extent, axis=along_axis)
    if side_code == 2:
        return lax.slice_in_dim(portion, 0, 1, axis=along_axis)
    return portion


def pick_rows(bricks, row_index):
    row_count = bricks.shape[0]
    clipped = jnp.where(row_index < row_count, row_index, row_count)
    padded_rows = jnp.concatenate([bricks, jnp.zeros((1,) + bricks.shape[1:], bricks.dtype)], 0)
    return padded_rows[clipped]


def fill_pool(voxel_field, send_x, send_y, brick_edge):
    slots, voxels, channels = voxel_field.shape
    bricks = voxel_field.reshape(slots, brick_edge, brick_edge, brick_edge, channels)
    gathered = [bricks]
    for lane_idx, shift_by, side_code in ((0, 1, 0), (1, -1, 2)):
        chosen = pick_rows(bricks, send_y[0, lane_idx])
        arrived = shifted(chosen, "gy", shift_by)
        gathered.append(arrived)
    first_section = jnp.concatenate(gathered, 0)
    pooled = [first_section]
    for lane_idx, shift_by, side_code in ((0, 1, 0), (1, -1, 2)):
        chosen = pick_rows(first_section, send_x[0, lane_idx])
        arrived = shifted(chosen, "gx", shift_by)
        pooled.append(arrived)
    pooled.append(jnp.zeros((1,) + bricks.shape[1:], bricks.dtype))
    return jnp.concatenate(pooled, 0)


def gather_block(pool_rows, neighbours):
    layers_x = []
    for off_x in range(3):
        layers_y = []
        for off_y in range(3):
            layers_z = []
            for off_z in range(3):
                portion = cut_layer(cut_layer(cut_layer(pool_rows, off_x, 1), off_y, 2), off_z, 3)
                layers_z.append(portion[neighbours[:, 9 * off_x + 3 * off_y + off_z]])
            layers_y.append(jnp.concatenate(layers_z, axis=3))
        layers_x.append(jnp.concatenate(layers_y, axis=2))
    return jnp.concatenate(layers_x, axis=1)


def to_columns(padded_block, brick_edge):
    tap_list = []
    for off_x in range(3):
        for off_y in range(3):
            for off_z in range(3):
                tap_list.append(
                    padded_block[
                        :,
                        off_x : off_x + brick_edge,
                        off_y : off_y + brick_edge,
                        off_z : off_z + brick_edge,
                    ]
                )
    stacked = jnp.stack(tap_list, axis=4)
    return stacked.reshape(-1, len(tap_list) * padded_block.shape[-1])


def transpose_conv(grad_field, weight, neighbours, send_x, send_y, brick_edge):
    slots, voxels, channels = grad_field.shape
    flipped = jnp.flip(weight, 0).transpose(0, 2, 1).reshape(-1, channels)
    pool_rows = fill_pool(grad_field, send_x, send_y, brick_edge)
    columns = to_columns(gather_block(pool_rows, neighbours), brick_edge)
    result = jnp.dot(columns, flipped, preferred_element_type=jnp.float32)
    return result.reshape(slots, voxels, channels)


def on_device(
    features, occupied, weight_one, bias_one, weight_two, cotangent, neighbours, send_x, send_y
):
    slots, voxels, channels = features.shape
    brick_edge = EDGE
    pool_end = slots + 2 * send_y.shape[2] + 2 * send_x.shape[2]
    live_bricks = (neighbours[:, 13] != pool_end).astype(jnp.int32)
    voxel_mask = (occupied * live_bricks[:, None]).astype(jnp.float32)[:, :, None]
    mask_half = voxel_mask.astype(jnp.bfloat16)
    masked = features * mask_half
    flat_one = weight_one.reshape(KVOL * channels, channels)
    flat_two = weight_two.reshape(KVOL * channels, channels)
    cols_input = to_columns(
        gather_block(fill_pool(masked, send_x, send_y, brick_edge), neighbours), brick_edge
    )
    preact = (
        jnp.dot(cols_input, flat_one, preferred_element_type=jnp.float32).reshape(
            slots, voxels, channels
        )
        + bias_one
    )
    hidden = (jax.nn.relu(preact) * voxel_mask).astype(jnp.bfloat16)
    cols_hidden = to_columns(
        gather_block(fill_pool(hidden, send_x, send_y, brick_edge), neighbours), brick_edge
    )
    second_conv = jnp.dot(cols_hidden, flat_two, preferred_element_type=jnp.float32).reshape(
        slots, voxels, channels
    )
    output = (second_conv * voxel_mask + masked.astype(jnp.float32)).astype(jnp.bfloat16)
    grad_out = cotangent * mask_half
    back_two = transpose_conv(grad_out, weight_two, neighbours, send_x, send_y, brick_edge)
    contract = (((0,), (0,)), ((), ()))
    sum_two = lax.dot_general(
        cols_hidden,
        grad_out.reshape(slots * voxels, channels),
        contract,
        preferred_element_type=jnp.float32,
    )
    grad_hidden = jnp.where(preact > 0, back_two * voxel_mask, 0.0).astype(jnp.bfloat16)
    back_one = transpose_conv(grad_hidden, weight_one, neighbours, send_x, send_y, brick_edge)
    sum_one = lax.dot_general(
        cols_input,
        grad_hidden.reshape(slots * voxels, channels),
        contract,
        preferred_element_type=jnp.float32,
    )
    sum_one, sum_two = lax.psum((sum_one, sum_two), ("gx", "gy"))
    grad_scale = 1.0 / math.sqrt(slots * voxels * lax.axis_size("gx") * lax.axis_size("gy"))
    grad_features = ((cotangent.astype(jnp.float32) + back_one) * voxel_mask).astype(jnp.bfloat16)
    grad_weight_one = (sum_one * grad_scale).reshape(KVOL, channels, channels)
    grad_weight_two = (sum_two * grad_scale).reshape(KVOL, channels, channels)
    return (output, grad_features, grad_weight_one, grad_weight_two)


def solution(mesh):
    in_specs = (
        P(("gx", "gy"), None, None),
        P(("gx", "gy"), None),
        P(),
        P(),
        P(),
        P(("gx", "gy"), None, None),
        P(("gx", "gy"), None),
        P(("gx", "gy"), None, None),
        P(("gx", "gy"), None, None),
    )
    out_specs = (P(("gx", "gy"), None, None), P(("gx", "gy"), None, None), P(), P())
    return jax.shard_map(
        on_device, mesh=mesh, in_specs=in_specs, out_specs=out_specs, check_vma=False
    )
```

profile of v0, /device:TPU:2, one launch (start us, length us, event | category | flops | bytes accessed | tf_op | source)
XLA Modules:
  0.0 849.3 jit_solution(8771616513204699121)
XLA Ops:
  13.2 9.1 %collective-permute-start = (bf16[2,8,8,8,128]{4,3,2,1,0:T(8,128)(2,1)}, bf16[2,8,8,8,128]{4,3,2,1,0:T(8,128)(2,1)S(1)}, u32[]{:S(2)}, u32[]{:S(2)}) collective-permute-start(bf16[2,8,8,8,128]{4,3,2,1,0:T(8,128)(2,1)} %gather_fusion), channel_id=1, source_target_pairs={{0,1},{1,2},{2,3},{3,4},{4,5},{5,6},{6,7},{8,9},{9,10},{10,11},{11... | collective-permute-start | bytes 786440 | tf_op jit(solution)/shard_map/ppermute | solution.py:14
  26.8 7.8 collective-permute-start.8
  35.9 2.8 collective-permute-start.9
  52.4 8.5 collective-permute-done.8
  60.8 9.4 %collective-permute-done.9 = bf16[2,8,8,8,128]{4,3,2,1,0:T(8,128)(2,1)S(1)} collective-permute-done((bf16[2,8,8,8,128]{4,3,2,1,0:T(8,128)(2,1)}, bf16[2,8,8,8,128]{4,3,2,1,0:T(8,128)(2,1)S(1)}, u32[]{:S(2)}, u32[]{:S(2)}) %collective-permute-start.9) | collective-permute-done | bytes 262176 | tf_op jit(solution)/shard_map/ppermute | solution.py:14
  72.5 2.2 collective-permute-start.2
  82.2 4.0 collective-permute-start.10
  90.6 2.1 constant_dynamic-update-slice_fusion.2
  97.5 2.3 fusion.60
  99.8 2.2 fusion.61
  106.0 2.3 fusion.62
  113.8 2.6 gather_fusion.79
  116.4 2.3 fusion.52
  118.7 2.3 fusion.53
  124.0 2.4 fusion.54
  187.9 2.0 gather_fusion.23
  189.9 2.0 gather_fusion.85
  198.1 2.0 gather_fusion.67
  201.7 2.0 gather_fusion.89
  205.0 2.0 gather_fusion.87
  209.9 2.0 gather_fusion.71
  213.2 2.0 gather_fusion.69
  218.1 2.0 gather_fusion.77
  221.4 2.0 gather_fusion.75
  226.3 2.0 gather_fusion.83
  233.0 2.3 gather_fusion.26
  235.2 2.2 gather_fusion.88
  237.5 2.3 gather_fusion.70
  257.5 4.1 copy.248
  283.6 4.7 copy.198
  288.4 4.6 multiply_convert_fusion
  301.1 6.5 collective-permute-start.12
  307.6 4.1 collective-permute-start.13
  311.7 5.6 collective-permute-start.4
  317.4 5.0 collective-permute-start.5
  325.2 20.1 %collective-permute-done.13 = bf16[2,8,8,8,128]{4,3,2,1,0:T(8,128)(2,1)S(1)} collective-permute-done((bf16[2,8,8,8,128]{4,3,2,1,0:T(8,128)(2,1)}, bf16[2,8,8,8,128]{4,3,2,1,0:T(8,128)(2,1)S(1)}, u32[]{:S(2)}, u32[]{:S(2)}) %collective-permute-start.13) | collective-permute-done | bytes 262176 | tf_op jit(solution)/shard_map/ppermute | solution.py:14
  345.4 11.2 %collective-permute-done.5 = bf16[2,8,8,8,128]{4,3,2,1,0:T(8,128)(2,1)} collective-permute-done((bf16[2,8,8,8,128]{4,3,2,1,0:T(8,128)(2,1)}, bf16[2,8,8,8,128]{4,3,2,1,0:T(8,128)(2,1)}, u32[]{:S(2)}, u32[]{:S(2)}) %collective-permute-start.5) | collective-permute-done | bytes 262176 | tf_op jit(solution)/shard_map/ppermute | solution.py:14
  359.5 2.9 collective-permute-start.6
  362.4 6.3 fusion.65
  376.6 3.1 collective-permute-start.14
  385.0 2.1 constant_dynamic-update-slice_fusion.35
  387.1 2.2 constant_dynamic-update-slice_fusion.34
  393.1 2.3 fusion.56
  395.3 2.2 fusion.57
  399.6 2.4 gather_fusion.48
  404.0 4.9 fusion.58
  416.1 2.4 fusion.50
  431.4 2.0 gather_fusion.54
  433.4 2.0 gather_fusion.60
  448.9 2.2 gather_fusion.57
  486.2 2.0 gather_fusion.104
  488.3 2.0 gather_fusion.116
  511.4 2.2 gather_fusion.119
  513.6 2.2 gather_fusion.101
  517.7 2.3 gather_fusion.109
  520.0 2.3 gather_fusion.107
  557.5 4.2 copy.223
  561.7 2.8 copy-done.1
  564.6 3.3 fusion.66
  570.2 4.7 copy.274
  575.0 4.0 fusion.5
  579.0 2.7 fusion.4
  581.7 256.3 %all-reduce.7.cloned.1.call-done = (f32[3456,128]{1,0:T(8,128)}, f32[3456,128]{1,0:T(8,128)}) async-done(((f32[3456,128]{1,0:T(8,128)}, f32[3456,128]{1,0:T(8,128)}), (f32[3456,128]{1,0:T(8,128)}, f32[3456,128]{1,0:T(8,128)})) %all-reduce.7.cloned.1.call-update) | async-done | bytes 3538960 | tf_op jit(solution)/shard_map/psum | solution.py:137
  838.0 2.9 broadcast_multiply_fusion.1
  (697 shorter events, 346.6 us)
Async XLA Ops:
  7.2 31.6 %copy-start.25 = (s32[2,27]{1,0:T(2,128)S(1)}, s32[2,27]{1,0:T(2,128)}, u32[]{:S(2)}) copy-start(s32[2,27]{1,0:T(2,128)} %param.15) | copy-start | bytes 652
  7.2 830.8 %all-reduce.7.cloned.1.call-start = ((), (), s32[]{:S(2)}) async-start(), calls=%async_computation | async-start | bytes 7077888 | tf_op jit(solution)/shard_map/psum | solution.py:137
  8.0 31.6 %copy-start.66 = (s32[1024]{0:T(1024)}, s32[1024]{0:T(1024)S(1)}, u32[]{:S(2)}) copy-start(s32[1024]{0:T(1024)S(1)} %pad_clamp_fusion.30) | copy-start | bytes 12292
  10.5 29.1 %copy-start.88 = (s32[1,2,6]{2,1,0:T(2,128)S(1)}, s32[1,2,6]{2,1,0:T(2,128)}, u32[]{:S(2)}) copy-start(s32[1,2,6]{2,1,0:T(2,128)} %param.16) | copy-start | bytes 148
  10.5 39.5 %copy-start.22 = (bf16[27,128,128]{2,1,0:T(8,128)(2,1)S(1)}, bf16[27,128,128]{2,1,0:T(8,128)(2,1)}, u32[]{:S(2)}) copy-start(bf16[27,128,128]{2,1,0:T(8,128)(2,1)} %param.13) | copy-start | bytes 2654212
  11.8 58.5 %copy-start.6 = (bf16[2,512,128]{2,1,0:T(8,128)(2,1)}, bf16[2,512,128]{2,1,0:T(8,128)(2,1)S(1)}, u32[]{:S(2)}) copy-start(bf16[2,512,128]{2,1,0:T(8,128)(2,1)S(1)} %get-tuple-element.125) | copy-start | bytes 786436
  13.2 39.2 %collective-permute-start = (bf16[2,8,8,8,128]{4,3,2,1,0:T(8,128)(2,1)}, bf16[2,8,8,8,128]{4,3,2,1,0:T(8,128)(2,1)S(1)}, u32[]{:S(2)}, u32[]{:S(2)}) collective-permute-start(bf16[2,8,8,8,128]{4,3,2,1,0:T(8,128)(2,1)} %gather_fusion), channel_id=1, source_target_pairs={{0,1},{1,2},{2,3},{3,4},{4,5},{5,6},{6,7},{8,9},{9,10},{10,11},{11... | collective-permute-start | bytes 786440 | tf_op jit(solution)/shard_map/ppermute | solution.py:14
  22.3 30.1 %copy-start.67 = (s32[1024]{0:T(1024)}, s32[1024]{0:T(1024)S(1)}, u32[]{:S(2)}) copy-start(s32[1024]{0:T(1024)S(1)} %pad_clamp_fusion.29) | copy-start | bytes 12292
  23.6 28.8 %collective-permute-start.1 = (bf16[2,8,8,8,128]{4,3,2,1,0:T(8,128)(2,1)}, bf16[2,8,8,8,128]{4,3,2,1,0:T(8,128)(2,1)S(1)}, u32[]{:S(2)}, u32[]{:S(2)}) collective-permute-start(bf16[2,8,8,8,128]{4,3,2,1,0:T(8,128)(2,1)} %gather_fusion.1), channel_id=1, source_target_pairs={{1,0},{2,1},{3,2},{4,3},{5,4},{6,5},{7,6},{9,8},{10,9},{11,10},{12... | collective-permute-start | bytes 786440 | tf_op jit(solution)/shard_map/ppermute | solution.py:14
  26.8 34.0 %collective-permute-start.8 = (bf16[2,8,8,8,128]{4,3,2,1,0:T(8,128)(2,1)}, bf16[2,8,8,8,128]{4,3,2,1,0:T(8,128)(2,1)S(1)}, u32[]{:S(2)}, u32[]{:S(2)}) collective-permute-start(bf16[2,8,8,8,128]{4,3,2,1,0:T(8,128)(2,1)} %gather_fusion.62), channel_id=1, source_target_pairs={{0,1},{1,2},{2,3},{3,4},{4,5},{5,6},{6,7},{8,9},{9,10},{10,11},{11... | collective-permute-start | bytes 786440 | tf_op jit(solution)/shard_map/ppermute | solution.py:14
  35.9 34.3 %collective-permute-start.9 = (bf16[2,8,8,8,128]{4,3,2,1,0:T(8,128)(2,1)}, bf16[2,8,8,8,128]{4,3,2,1,0:T(8,128)(2,1)S(1)}, u32[]{:S(2)}, u32[]{:S(2)}) collective-permute-start(bf16[2,8,8,8,128]{4,3,2,1,0:T(8,128)(2,1)} %gather_fusion.63), channel_id=1, source_target_pairs={{1,0},{2,1},{3,2},{4,3},{5,4},{6,5},{7,6},{9,8},{10,9},{11,10},{12... | collective-permute-start | bytes 786440 | tf_op jit(solution)/shard_map/ppermute | solution.py:14
  44.0 106.9 %copy-start.65 = (s32[1024]{0:T(1024)}, s32[1024]{0:T(1024)S(1)}, u32[]{:S(2)}) copy-start(s32[1024]{0:T(1024)S(1)} %get-tuple-element.180) | copy-start | bytes 12292
  50.0 30.5 %copy-start.68 = (s32[1024]{0:T(1024)}, s32[1024]{0:T(1024)S(1)}, u32[]{:S(2)}) copy-start(s32[1024]{0:T(1024)S(1)} %pad_clamp_fusion.28) | copy-start | bytes 12292
  72.5 18.1 %collective-permute-start.2 = (bf16[6,8,8,8,128]{4,3,2,1,0:T(8,128)(2,1)}, bf16[6,8,8,8,128]{4,3,2,1,0:T(8,128)(2,1)}, u32[]{:S(2)}, u32[]{:S(2)}) collective-permute-start(bf16[6,8,8,8,128]{4,3,2,1,0:T(8,128)(2,1)} %gather_fusion.2), channel_id=1, source_target_pairs={{0,8},{8,16},{16,24},{24,32},{32,40},{40,48},{48,56},{56,64},{64,7... | collective-permute-start | bytes 2359304 | tf_op jit(solution)/shard_map/ppermute | solution.py:14
  74.7 7.5 copy-start.69
  76.3 16.4 %collective-permute-start.3 = (bf16[6,8,8,8,128]{4,3,2,1,0:T(8,128)(2,1)}, bf16[6,8,8,8,128]{4,3,2,1,0:T(8,128)(2,1)S(1)}, u32[]{:S(2)}, u32[]{:S(2)}) collective-permute-start(bf16[6,8,8,8,128]{4,3,2,1,0:T(8,128)(2,1)} %gather_fusion.3), channel_id=1, source_target_pairs={{8,0},{16,8},{24,16},{32,24},{40,32},{48,40},{56,48},{64,56},{72,6... | collective-permute-start | bytes 2359304 | tf_op jit(solution)/shard_map/ppermute | solution.py:14
  82.2 21.7 %collective-permute-start.10 = (bf16[6,8,8,8,128]{4,3,2,1,0:T(8,128)(2,1)}, bf16[6,8,8,8,128]{4,3,2,1,0:T(8,128)(2,1)S(1)}, u32[]{:S(2)}, u32[]{:S(2)}) collective-permute-start(bf16[6,8,8,8,128]{4,3,2,1,0:T(8,128)(2,1)} %gather_fusion.64), channel_id=1, source_target_pairs={{0,8},{8,16},{16,24},{24,32},{32,40},{40,48},{48,56},{56,64},{64,7... | collective-permute-start | bytes 2359304 | tf_op jit(solution)/shard_map/ppermute | solution.py:14
  86.2 22.1 %collective-permute-start.11 = (bf16[6,8,8,8,128]{4,3,2,1,0:T(8,128)(2,1)}, bf16[6,8,8,8,128]{4,3,2,1,0:T(8,128)(2,1)S(1)}, u32[]{:S(2)}, u32[]{:S(2)}) collective-permute-start(bf16[6,8,8,8,128]{4,3,2,1,0:T(8,128)(2,1)} %gather_fusion.65), channel_id=1, source_target_pairs={{8,0},{16,8},{24,16},{32,24},{40,32},{48,40},{56,48},{64,56},{72,6... | collective-permute-start | bytes 2359304 | tf_op jit(solution)/shard_map/ppermute | solution.py:14
  94.3 10.6 %copy-start.3 = (bf16[19,8,8,8,128]{4,3,2,1,0:T(8,128)(2,1)S(1)}, bf16[19,8,8,8,128]{4,3,2,1,0:T(8,128)(2,1)}, u32[]{:S(2)}) copy-start(bf16[19,8,8,8,128]{4,3,2,1,0:T(8,128)(2,1)} %constant_dynamic-update-slice_fusion) | copy-start | bytes 7471108
  113.8 9.1 %copy-start.5 = (bf16[19,8,8,8,128]{4,3,2,1,0:T(8,128)(2,1)S(1)}, bf16[19,8,8,8,128]{4,3,2,1,0:T(8,128)(2,1)}, u32[]{:S(2)}) copy-start(bf16[19,8,8,8,128]{4,3,2,1,0:T(8,128)(2,1)} %constant_dynamic-update-slice_fusion.66) | copy-start | bytes 7471108
  145.2 10.7 %copy-start.32 = (bf16[2,8,1,1,128]{4,3,2,1,0:T(2,128)(2,1)}, bf16[2,8,1,1,128]{4,3,2,1,0:T(2,128)(2,1)S(1)}, u32[]{:S(2)}) copy-start(bf16[2,8,1,1,128]{4,3,2,1,0:T(2,128)(2,1)S(1)} %copy.177) | copy-start | bytes 12292
  145.9 10.0 %copy-start.34 = (bf16[2,8,1,1,128]{4,3,2,1,0:T(2,128)(2,1)}, bf16[2,8,1,1,128]{4,3,2,1,0:T(2,128)(2,1)S(1)}, u32[]{:S(2)}) copy-start(bf16[2,8,1,1,128]{4,3,2,1,0:T(2,128)(2,1)S(1)} %copy.176) | copy-start | bytes 12292
  155.8 84.0 %copy-start.8 = (bf16[19,8,8,1,128]{4,3,2,1,0:T(2,128)(2,1)S(1)}, bf16[19,8,8,1,128]{4,3,2,1,0:T(2,128)(2,1)}, u32[]{:S(2)}) copy-start(bf16[19,8,8,1,128]{4,3,2,1,0:T(2,128)(2,1)} %get-tuple-element.58) | copy-start | bytes 933892
  268.7 7.2 copy-start.29
  268.7 7.2 copy-start.33
  268.7 7.2 copy-start.35
  268.7 7.2 copy-start.49
  268.7 7.2 copy-start.50
  268.7 7.2 copy-start.59
  268.8 7.2 copy-start.60
  268.8 7.2 copy-start.72
  268.8 7.2 copy-start.73
  268.8 7.2 copy-start.74
  268.8 7.2 copy-start.75
  282.8 10.2 %slice-start.2 = ((s8[7077888]{0:T(1024)(128)(4,1)}), s8[4194304]{0:T(1024)(128)(4,1)S(1)}, s32[]{:S(2)}) async-start(s8[7077888]{0:T(1024)(128)(4,1)} %bitcast.920), calls=%async_computation.3 | async-start | bytes 8388608
  283.6 9.4 %slice-start.3 = ((s8[7077888]{0:T(1024)(128)(4,1)}), s8[2883584]{0:T(1024)(128)(4,1)S(1)}, s32[]{:S(2)}) async-start(s8[7077888]{0:T(1024)(128)(4,1)} %bitcast.920), calls=%async_computation.4 | async-start | bytes 5767168
  295.1 27.3 %copy-start.21 = (bf16[27,128,128]{2,1,0:T(8,128)(2,1)S(1)}, bf16[27,128,128]{2,1,0:T(8,128)(2,1)}, u32[]{:S(2)}) copy-start(bf16[27,128,128]{2,1,0:T(8,128)(2,1)} %param.11) | copy-start | bytes 2654212
  298.1 58.6 %copy-start.18 = (bf16[1,8,8,8,128]{4,3,2,1,0:T(8,128)(2,1)S(1)}, bf16[1,8,8,8,128]{4,3,2,1,0:T(8,128)(2,1)}, u32[]{:S(2)}) copy-start(bf16[1,8,8,8,128]{4,3,2,1,0:T(8,128)(2,1)} %copy-done.17) | copy-start | bytes 393220
  301.1 24.1 %collective-permute-start.12 = (bf16[2,8,8,8,128]{4,3,2,1,0:T(8,128)(2,1)}, bf16[2,8,8,8,128]{4,3,2,1,0:T(8,128)(2,1)S(1)}, u32[]{:S(2)}, u32[]{:S(2)}) collective-permute-start(bf16[2,8,8,8,128]{4,3,2,1,0:T(8,128)(2,1)} %gather_fusion.93), channel_id=1, source_target_pairs={{0,1},{1,2},{2,3},{3,4},{4,5},{5,6},{6,7},{8,9},{9,10},{10,11},{11... | collective-permute-start | bytes 786440 | tf_op jit(solution)/shard_map/ppermute | solution.py:14
  307.6 37.7 %collective-permute-start.13 = (bf16[2,8,8,8,128]{4,3,2,1,0:T(8,128)(2,1)}, bf16[2,8,8,8,128]{4,3,2,1,0:T(8,128)(2,1)S(1)}, u32[]{:S(2)}, u32[]{:S(2)}) collective-permute-start(bf16[2,8,8,8,128]{4,3,2,1,0:T(8,128)(2,1)} %gather_fusion.94), channel_id=1, source_target_pairs={{1,0},{2,1},{3,2},{4,3},{5,4},{6,5},{7,6},{9,8},{10,9},{11,10},{12... | collective-permute-start | bytes 786440 | tf_op jit(solution)/shard_map/ppermute | solution.py:14
  311.7 33.7 %collective-permute-start.4 = (bf16[2,8,8,8,128]{4,3,2,1,0:T(8,128)(2,1)}, bf16[2,8,8,8,128]{4,3,2,1,0:T(8,128)(2,1)S(1)}, u32[]{:S(2)}, u32[]{:S(2)}) collective-permute-start(bf16[2,8,8,8,128]{4,3,2,1,0:T(8,128)(2,1)} %gather_fusion.31), channel_id=1, source_target_pairs={{0,1},{1,2},{2,3},{3,4},{4,5},{5,6},{6,7},{8,9},{9,10},{10,11},{11... | collective-permute-start | bytes 786440 | tf_op jit(solution)/shard_map/ppermute | solution.py:14
  317.4 39.3 %collective-permute-start.5 = (bf16[2,8,8,8,128]{4,3,2,1,0:T(8,128)(2,1)}, bf16[2,8,8,8,128]{4,3,2,1,0:T(8,128)(2,1)}, u32[]{:S(2)}, u32[]{:S(2)}) collective-permute-start(bf16[2,8,8,8,128]{4,3,2,1,0:T(8,128)(2,1)} %gather_fusion.32), channel_id=1, source_target_pairs={{1,0},{2,1},{3,2},{4,3},{5,4},{6,5},{7,6},{9,8},{10,9},{11,10},{12... | collective-permute-start | bytes 786440 | tf_op jit(solution)/shard_map/ppermute | solution.py:14
  359.5 25.5 %collective-permute-start.6 = (bf16[6,8,8,8,128]{4,3,2,1,0:T(8,128)(2,1)}, bf16[6,8,8,8,128]{4,3,2,1,0:T(8,128)(2,1)}, u32[]{:S(2)}, u32[]{:S(2)}) collective-permute-start(bf16[6,8,8,8,128]{4,3,2,1,0:T(8,128)(2,1)} %gather_fusion.33), channel_id=1, source_target_pairs={{0,8},{8,16},{16,24},{24,32},{32,40},{40,48},{48,56},{56,64},{64,7... | collective-permute-start | bytes 2359304 | tf_op jit(solution)/shard_map/ppermute | solution.py:14
  370.3 16.7 %collective-permute-start.7 = (bf16[6,8,8,8,128]{4,3,2,1,0:T(8,128)(2,1)}, bf16[6,8,8,8,128]{4,3,2,1,0:T(8,128)(2,1)}, u32[]{:S(2)}, u32[]{:S(2)}) collective-permute-start(bf16[6,8,8,8,128]{4,3,2,1,0:T(8,128)(2,1)} %gather_fusion.34), channel_id=1, source_target_pairs={{8,0},{16,8},{24,16},{32,24},{40,32},{48,40},{56,48},{64,56},{72,6... | collective-permute-start | bytes 2359304 | tf_op jit(solution)/shard_map/ppermute | solution.py:14
  376.6 22.9 %collective-permute-start.14 = (bf16[6,8,8,8,128]{4,3,2,1,0:T(8,128)(2,1)}, bf16[6,8,8,8,128]{4,3,2,1,0:T(8,128)(2,1)S(1)}, u32[]{:S(2)}, u32[]{:S(2)}) collective-permute-start(bf16[6,8,8,8,128]{4,3,2,1,0:T(8,128)(2,1)} %gather_fusion.95), channel_id=1, source_target_pairs={{0,8},{8,16},{16,24},{24,32},{32,40},{40,48},{48,56},{56,64},{64,7... | collective-permute-start | bytes 2359304 | tf_op jit(solution)/shard_map/ppermute | solution.py:14
  379.6 29.3 %collective-permute-start.15 = (bf16[6,8,8,8,128]{4,3,2,1,0:T(8,128)(2,1)}, bf16[6,8,8,8,128]{4,3,2,1,0:T(8,128)(2,1)}, u32[]{:S(2)}, u32[]{:S(2)}) collective-permute-start(bf16[6,8,8,8,128]{4,3,2,1,0:T(8,128)(2,1)} %gather_fusion.96), channel_id=1, source_target_pairs={{8,0},{16,8},{24,16},{32,24},{40,32},{48,40},{56,48},{64,56},{72,6... | collective-permute-start | bytes 2359304 | tf_op jit(solution)/shard_map/ppermute | solution.py:14
  387.1 12.5 %copy-start.4 = (bf16[19,8,8,8,128]{4,3,2,1,0:T(8,128)(2,1)S(1)}, bf16[19,8,8,8,128]{4,3,2,1,0:T(8,128)(2,1)}, u32[]{:S(2)}) copy-start(bf16[19,8,8,8,128]{4,3,2,1,0:T(8,128)(2,1)} %constant_dynamic-update-slice_fusion.102) | copy-start | bytes 7471108
  418.5 39.6 %copy-start.10 = (bf16[19,8,8,1,128]{4,3,2,1,0:T(2,128)(2,1)S(1)}, bf16[19,8,8,1,128]{4,3,2,1,0:T(2,128)(2,1)}, u32[]{:S(2)}) copy-start(bf16[19,8,8,1,128]{4,3,2,1,0:T(2,128)(2,1)} %get-tuple-element.85) | copy-start | bytes 933892
  453.9 23.9 %copy-start.47 = (bf16[19,1,1,1,128]{4,3,2,1,0:T(2,128)(2,1)S(1)}, bf16[19,1,1,1,128]{4,3,2,1,0:T(2,128)(2,1)}, u32[]{:S(2)}) copy-start(bf16[19,1,1,1,128]{4,3,2,1,0:T(2,128)(2,1)} %get-tuple-element.12) | copy-start | bytes 14596
  453.9 26.5 %copy-start.46 = (bf16[19,1,1,1,128]{4,3,2,1,0:T(2,128)(2,1)S(1)}, bf16[19,1,1,1,128]{4,3,2,1,0:T(2,128)(2,1)}, u32[]{:S(2)}) copy-start(bf16[19,1,1,1,128]{4,3,2,1,0:T(2,128)(2,1)} %get-tuple-element.13) | copy-start | bytes 14596
  453.9 27.7 %copy-start.45 = (bf16[19,1,1,1,128]{4,3,2,1,0:T(2,128)(2,1)S(1)}, bf16[19,1,1,1,128]{4,3,2,1,0:T(2,128)(2,1)}, u32[]{:S(2)}) copy-start(bf16[19,1,1,1,128]{4,3,2,1,0:T(2,128)(2,1)} %get-tuple-element.14) | copy-start | bytes 14596
  453.9 29.0 %copy-start.44 = (bf16[19,1,1,1,128]{4,3,2,1,0:T(2,128)(2,1)S(1)}, bf16[19,1,1,1,128]{4,3,2,1,0:T(2,128)(2,1)}, u32[]{:S(2)}) copy-start(bf16[19,1,1,1,128]{4,3,2,1,0:T(2,128)(2,1)} %get-tuple-element.15) | copy-start | bytes 14596
  458.9 58.8 %copy-start.13 = (bf16[2,8,8,1,128]{4,3,2,1,0:T(2,128)(2,1)}, bf16[2,8,8,1,128]{4,3,2,1,0:T(2,128)(2,1)S(1)}, u32[]{:S(2)}) copy-start(bf16[2,8,8,1,128]{4,3,2,1,0:T(2,128)(2,1)S(1)} %copy.209) | copy-start | bytes 98308
  459.1 65.7 %copy-start.9 = (bf16[19,8,8,1,128]{4,3,2,1,0:T(2,128)(2,1)S(1)}, bf16[19,8,8,1,128]{4,3,2,1,0:T(2,128)(2,1)}, u32[]{:S(2)}) copy-start(bf16[19,8,8,1,128]{4,3,2,1,0:T(2,128)(2,1)} %get-tuple-element.33) | copy-start | bytes 933892
  504.8 26.0 %copy-start.36 = (bf16[2,8,1,1,128]{4,3,2,1,0:T(2,128)(2,1)}, bf16[2,8,1,1,128]{4,3,2,1,0:T(2,128)(2,1)S(1)}, u32[]{:S(2)}) copy-start(bf16[2,8,1,1,128]{4,3,2,1,0:T(2,128)(2,1)S(1)} %copy.262) | copy-start | bytes 12292
  507.8 23.0 %copy-start.38 = (bf16[2,8,1,1,128]{4,3,2,1,0:T(2,128)(2,1)}, bf16[2,8,1,1,128]{4,3,2,1,0:T(2,128)(2,1)S(1)}, u32[]{:S(2)}) copy-start(bf16[2,8,1,1,128]{4,3,2,1,0:T(2,128)(2,1)S(1)} %copy.261) | copy-start | bytes 12292
  524.7 7.6 copy-start.15
  534.7 22.0 %copy-start.2 = (bf16[2,8,8,8,27,128]{5,3,2,1,0,4:T(8,128)(2,1)}, bf16[2,8,8,8,27,128]{5,3,2,1,0,4:T(8,128)(2,1)S(1)}, u32[]{:S(2)}) copy-start(bf16[2,8,8,8,27,128]{5,3,2,1,0,4:T(8,128)(2,1)S(1)} %constant_dynamic-update-slice_fusion.108) | copy-start | bytes 21233668
  542.6 7.2 copy-start.57
  542.6 7.2 copy-start.58
  542.7 7.2 copy-start.76
  542.7 7.2 copy-start.77
  569.4 9.6 %slice-start = ((s8[7077888]{0:T(1024)(128)(4,1)}), s8[4194304]{0:T(1024)(128)(4,1)S(1)}, s32[]{:S(2)}) async-start(s8[7077888]{0:T(1024)(128)(4,1)} %bitcast.917), calls=%async_computation.1 | async-start | bytes 8388608
  570.2 8.8 %slice-start.1 = ((s8[7077888]{0:T(1024)(128)(4,1)}), s8[2883584]{0:T(1024)(128)(4,1)S(1)}, s32[]{:S(2)}) async-start(s8[7077888]{0:T(1024)(128)(4,1)} %bitcast.917), calls=%async_computation.2 | async-start | bytes 5767168
  (47 other events, 144.5 us)
Sparse Core Ops, SparseCore 0:
  568.0 270.0 all-reduce.6
where the time goes:
time: 861 us; the launch traced here: 849 us
  local copies, waits for them, and re-layouts  408 us (47%)
  waiting for transfers between devices  306 us (36%)
  starting transfers between devices  60.5 us (7%)
  other arithmetic  35.3 us (4%)
  matrix products  22.9 us (3%)
  between operations  16.4 us (2%)
    psum x1, waiting for transfers between devices, on_device(): sum_one, sum_two = lax.psum((sum_one, sum_two), ('gx', 'gy'))  256 us
    gather x180, local copies, waits for them, and re-layouts, gather_block(): layers_z.append(portion[neighbours[:, 9 * off_x + 3 * off_y + off_z]])  186 us
    unnamed x387, local copies, waits for them, and re-layouts  122 us
    ppermute x16, starting transfers between devices, shifted(): return lax.ppermute(block, axis, route)  60.5 us
    ppermute x16, waiting for transfers between devices, shifted(): return lax.ppermute(block, axis, route)  49.9 us
    slice x24, local copies, waits for them, and re-layouts, cut_layer(): return lax.slice_in_dim(portion, extent - 1, extent, axis=along_axis)  43.2 us
    gather x16, local copies, waits for them, and re-layouts, pick_rows(): return padded_rows[clipped]  24.3 us
    another operation x8, local copies, waits for them, and re-layouts, to_columns(): stacked = jnp.stack(tap_list, axis=4)  20.3 us
  transfers between devices with their start and end apart: 17, of which 7 were waited for; matrix products, arithmetic and copies ran while one was open for 12% of the time, Pallas kernels for 0%

commit v1 on v0

--- a/solution.py
+++ b/solution.py
@@ -6,6 +6,11 @@
 
 EDGE = 8
 KVOL = 27
+
+
+def axis_by_axis(value, axis_one, axis_two):
+    inner = lax.psum(value, axis_one)
+    return lax.psum(inner, axis_two)
 
 
 def shifted(block, axis, distance):
@@ -134,7 +139,7 @@
         contract,
         preferred_element_type=jnp.float32,
     )
-    sum_one, sum_two = lax.psum((sum_one, sum_two), ("gx", "gy"))
+    sum_one, sum_two = axis_by_axis((sum_one, sum_two), "gx", "gy")
     grad_scale = 1.0 / math.sqrt(slots * voxels * lax.axis_size("gx") * lax.axis_size("gy"))
     grad_features = ((cotangent.astype(jnp.float32) + back_one) * voxel_mask).astype(jnp.bfloat16)
     grad_weight_one = (sum_one * grad_scale).reshape(KVOL, channels, channels)

time: 861 us -> 1150 us (1.34)
  waiting for transfers between devices: 306 us -> 603 us
    psum x1 -> x2, waiting for transfers between devices: 256 us -> 553 us  [the longest x1 277 us: axis_by_axis(): inner = lax.psum(value, axis_one)]
    gather x180, local copies, waits for them, and re-layouts: 186 us -> 170 us  [gather_block(): layers_z.append(portion[neighbours[:, 9 * off_x + 3 * off_y + off_z]])]
    unnamed x387 -> x383, local copies, waits for them, and re-layouts: 122 us -> 130 us
  transfers between devices with their start and end apart: 17 -> 18, of which waited for: 7 -> 8; matrix products, arithmetic and copies ran while one was open for 12% -> 11% of each run, Pallas kernels for 0% -> 0%
where the time goes in v1:
time: 1150 us; the launch traced here: 1140 us
  waiting for transfers between devices  603 us (52%)
  local copies, waits for them, and re-layouts  400 us (35%)
  starting transfers between devices  60.6 us (5%)
  other arithmetic  36.8 us (3%)
  matrix products  22.9 us (2%)
  between operations  16.2 us (1%)
    psum x1, waiting for transfers between devices, axis_by_axis(): inner = lax.psum(value, axis_one)  277 us
    psum x1, waiting for transfers between devices, axis_by_axis(): return lax.psum(inner, axis_two)  276 us
    gather x180, local copies, waits for them, and re-layouts, gather_block(): layers_z.append(portion[neighbours[:, 9 * off_x + 3 * off_y + off_z]])  170 us
    unnamed x383, local copies, waits for them, and re-layouts  130 us
    ppermute x16, starting transfers between devices, shifted(): return lax.ppermute(block, axis, route)  60.5 us
    ppermute x16, waiting for transfers between devices, shifted(): return lax.ppermute(block, axis, route)  49.9 us
    slice x24, local copies, waits for them, and re-layouts, cut_layer(): return lax.slice_in_dim(portion, extent - 1, extent, axis=along_axis)  43.2 us
    gather x16, local copies, waits for them, and re-layouts, pick_rows(): return padded_rows[clipped]  24.2 us
  transfers between devices with their start and end apart: 18, of which 8 were waited for; matrix products, arithmetic and copies ran while one was open for 11% of the time, Pallas kernels for 0%

profile of v1, /device:TPU:2, one launch (start us, length us, event | category | flops | bytes accessed | tf_op | source)
XLA Modules:
  0.0 1139.4 jit_solution(6604949132598571599)
XLA Ops:
  13.2 9.1 collective-permute-start
  26.8 7.8 collective-permute-start.8
  35.9 2.8 collective-permute-start.9
  52.4 8.5 collective-permute-done.8
  60.8 9.4 collective-permute-done.9
  72.5 2.2 collective-permute-start.2
  82.2 4.0 collective-permute-start.10
  90.6 2.1 constant_dynamic-update-slice_fusion.2
  97.5 2.3 fusion.60
  99.8 2.2 fusion.61
  106.0 2.3 fusion.62
  113.8 2.6 gather_fusion.79
  116.4 2.3 fusion.52
  118.6 2.3 fusion.53
  123.9 2.4 fusion.54
  187.7 2.0 gather_fusion.23
  189.7 2.0 gather_fusion.85
  191.8 2.0 gather_fusion.29
  193.8 2.0 gather_fusion.91
  197.9 2.0 gather_fusion.67
  201.5 2.0 gather_fusion.89
  204.8 2.0 gather_fusion.87
  209.7 2.0 gather_fusion.71
  213.0 2.0 gather_fusion.69
  217.9 2.0 gather_fusion.77
  221.2 2.0 gather_fusion.75
  226.1 2.0 gather_fusion.83
  229.4 2.0 gather_fusion.81
  232.7 2.3 gather_fusion.26
  235.0 2.2 gather_fusion.88
  237.2 2.3 gather_fusion.70
  257.3 4.1 copy.248
  283.4 4.7 copy.198
  288.2 4.6 multiply_convert_fusion
  300.8 6.5 collective-permute-start.12
  307.4 4.1 collective-permute-start.13
  311.5 5.6 collective-permute-start.4
  317.1 5.0 collective-permute-start.5
  325.0 20.1 %collective-permute-done.13 = bf16[2,8,8,8,128]{4,3,2,1,0:T(8,128)(2,1)S(1)} collective-permute-done((bf16[2,8,8,8,128]{4,3,2,1,0:T(8,128)(2,1)}, bf16[2,8,8,8,128]{4,3,2,1,0:T(8,128)(2,1)S(1)}, u32[]{:S(2)}, u32[]{:S(2)}) %collective-permute-start.13) | collective-permute-done | bytes 262176 | tf_op jit(solution)/shard_map/ppermute | solution.py:19
  345.2 11.2 collective-permute-done.5
  359.3 2.9 collective-permute-start.6
  362.1 6.3 fusion.65
  376.3 3.1 collective-permute-start.14
  384.7 2.1 constant_dynamic-update-slice_fusion.35
  386.8 2.2 constant_dynamic-update-slice_fusion.34
  392.8 2.3 fusion.56
  395.1 2.2 fusion.57
  399.4 2.4 gather_fusion.48
  403.8 4.9 fusion.58
  415.9 2.4 fusion.50
  431.1 2.0 gather_fusion.54
  433.1 2.0 gather_fusion.60
  450.2 2.2 gather_fusion.57
  467.3 2.0 gather_fusion.98
  469.4 2.0 gather_fusion.104
  523.3 4.2 copy.223
  527.6 2.9 copy-done
  530.5 3.3 fusion.66
  546.5 276.8 %all-reduce.9.cloned.1.call-done = (f32[3456,128]{1,0:T(8,128)}, f32[3456,128]{1,0:T(8,128)}) async-done(((f32[3456,128]{1,0:T(8,128)}, f32[3456,128]{1,0:T(8,128)}), (f32[3456,128]{1,0:T(8,128)}, f32[3456,128]{1,0:T(8,128)})) %all-reduce.9.cloned.1.call-update) | async-done | bytes 3538960 | tf_op jit(solution)/shard_map/psum | solution.py:12
  840.6 4.7 copy.274
  845.4 4.0 fusion.5
  849.4 2.7 fusion.4
  852.1 276.0 %all-reduce.11.cloned.1.call-done = (f32[3456,128]{1,0:T(8,128)}, f32[3456,128]{1,0:T(8,128)}) async-done(((f32[3456,128]{1,0:T(8,128)}, f32[3456,128]{1,0:T(8,128)}), (f32[3456,128]{1,0:T(8,128)}, f32[3456,128]{1,0:T(8,128)})) %all-reduce.11.cloned.1.call-update) | async-done | bytes 3538960 | tf_op jit(solution)/shard_map/psum | solution.py:13
  1128.1 2.9 broadcast_multiply_fusion.1
  (696 shorter events, 343.1 us)
Async XLA Ops:
  7.2 31.6 %copy-start.30 = (s32[2,27]{1,0:T(2,128)S(1)}, s32[2,27]{1,0:T(2,128)}, u32[]{:S(2)}) copy-start(s32[2,27]{1,0:T(2,128)} %param.15) | copy-start | bytes 652
  7.2 816.2 %all-reduce.9.cloned.1.call-start = ((), (), s32[]{:S(2)}) async-start(), calls=%async_computation | async-start | bytes 7077888 | tf_op jit(solution)/shard_map/psum | solution.py:12
  8.0 31.6 %copy-start.68 = (s32[1024]{0:T(1024)}, s32[1024]{0:T(1024)S(1)}, u32[]{:S(2)}) copy-start(s32[1024]{0:T(1024)S(1)} %pad_clamp_fusion.30) | copy-start | bytes 12292
  10.5 29.1 %copy-start.86 = (s32[1,2,6]{2,1,0:T(2,128)S(1)}, s32[1,2,6]{2,1,0:T(2,128)}, u32[]{:S(2)}) copy-start(s32[1,2,6]{2,1,0:T(2,128)} %param.16) | copy-start | bytes 148
  10.5 39.5 %copy-start.27 = (bf16[27,128,128]{2,1,0:T(8,128)(2,1)S(1)}, bf16[27,128,128]{2,1,0:T(8,128)(2,1)}, u32[]{:S(2)}) copy-start(bf16[27,128,128]{2,1,0:T(8,128)(2,1)} %param.13) | copy-start | bytes 2654212
  11.8 58.5 %copy-start.5 = (bf16[2,512,128]{2,1,0:T(8,128)(2,1)}, bf16[2,512,128]{2,1,0:T(8,128)(2,1)S(1)}, u32[]{:S(2)}) copy-start(bf16[2,512,128]{2,1,0:T(8,128)(2,1)S(1)} %get-tuple-element.127) | copy-start | bytes 786436
  13.2 39.2 %collective-permute-start = (bf16[2,8,8,8,128]{4,3,2,1,0:T(8,128)(2,1)}, bf16[2,8,8,8,128]{4,3,2,1,0:T(8,128)(2,1)S(1)}, u32[]{:S(2)}, u32[]{:S(2)}) collective-permute-start(bf16[2,8,8,8,128]{4,3,2,1,0:T(8,128)(2,1)} %gather_fusion), channel_id=1, source_target_pairs={{0,1},{1,2},{2,3},{3,4},{4,5},{5,6},{6,7},{8,9},{9,10},{10,11},{11... | collective-permute-start | bytes 786440 | tf_op jit(solution)/shard_map/ppermute | solution.py:19
  22.3 30.1 %copy-start.69 = (s32[1024]{0:T(1024)}, s32[1024]{0:T(1024)S(1)}, u32[]{:S(2)}) copy-start(s32[1024]{0:T(1024)S(1)} %pad_clamp_fusion.29) | copy-start | bytes 12292
  23.6 28.8 %collective-permute-start.1 = (bf16[2,8,8,8,128]{4,3,2,1,0:T(8,128)(2,1)}, bf16[2,8,8,8,128]{4,3,2,1,0:T(8,128)(2,1)S(1)}, u32[]{:S(2)}, u32[]{:S(2)}) collective-permute-start(bf16[2,8,8,8,128]{4,3,2,1,0:T(8,128)(2,1)} %gather_fusion.1), channel_id=1, source_target_pairs={{1,0},{2,1},{3,2},{4,3},{5,4},{6,5},{7,6},{9,8},{10,9},{11,10},{12... | collective-permute-start | bytes 786440 | tf_op jit(solution)/shard_map/ppermute | solution.py:19
  26.8 34.0 %collective-permute-start.8 = (bf16[2,8,8,8,128]{4,3,2,1,0:T(8,128)(2,1)}, bf16[2,8,8,8,128]{4,3,2,1,0:T(8,128)(2,1)S(1)}, u32[]{:S(2)}, u32[]{:S(2)}) collective-permute-start(bf16[2,8,8,8,128]{4,3,2,1,0:T(8,128)(2,1)} %gather_fusion.62), channel_id=1, source_target_pairs={{0,1},{1,2},{2,3},{3,4},{4,5},{5,6},{6,7},{8,9},{9,10},{10,11},{11... | collective-permute-start | bytes 786440 | tf_op jit(solution)/shard_map/ppermute | solution.py:19
  35.9 34.3 %collective-permute-start.9 = (bf16[2,8,8,8,128]{4,3,2,1,0:T(8,128)(2,1)}, bf16[2,8,8,8,128]{4,3,2,1,0:T(8,128)(2,1)S(1)}, u32[]{:S(2)}, u32[]{:S(2)}) collective-permute-start(bf16[2,8,8,8,128]{4,3,2,1,0:T(8,128)(2,1)} %gather_fusion.63), channel_id=1, source_target_pairs={{1,0},{2,1},{3,2},{4,3},{5,4},{6,5},{7,6},{9,8},{10,9},{11,10},{12... | collective-permute-start | bytes 786440 | tf_op jit(solution)/shard_map/ppermute | solution.py:19
  44.0 106.9 %copy-start.67 = (s32[1024]{0:T(1024)}, s32[1024]{0:T(1024)S(1)}, u32[]{:S(2)}) copy-start(s32[1024]{0:T(1024)S(1)} %get-tuple-element.182) | copy-start | bytes 12292
  50.0 30.5 %copy-start.70 = (s32[1024]{0:T(1024)}, s32[1024]{0:T(1024)S(1)}, u32[]{:S(2)}) copy-start(s32[1024]{0:T(1024)S(1)} %pad_clamp_fusion.28) | copy-start | bytes 12292
  72.5 18.1 %collective-permute-start.2 = (bf16[6,8,8,8,128]{4,3,2,1,0:T(8,128)(2,1)}, bf16[6,8,8,8,128]{4,3,2,1,0:T(8,128)(2,1)}, u32[]{:S(2)}, u32[]{:S(2)}) collective-permute-start(bf16[6,8,8,8,128]{4,3,2,1,0:T(8,128)(2,1)} %gather_fusion.2), channel_id=1, source_target_pairs={{0,8},{8,16},{16,24},{24,32},{32,40},{40,48},{48,56},{56,64},{64,7... | collective-permute-start | bytes 2359304 | tf_op jit(solution)/shard_map/ppermute | solution.py:19
  74.7 7.5 copy-start.71
  76.3 16.4 %collective-permute-start.3 = (bf16[6,8,8,8,128]{4,3,2,1,0:T(8,128)(2,1)}, bf16[6,8,8,8,128]{4,3,2,1,0:T(8,128)(2,1)S(1)}, u32[]{:S(2)}, u32[]{:S(2)}) collective-permute-start(bf16[6,8,8,8,128]{4,3,2,1,0:T(8,128)(2,1)} %gather_fusion.3), channel_id=1, source_target_pairs={{8,0},{16,8},{24,16},{32,24},{40,32},{48,40},{56,48},{64,56},{72,6... | collective-permute-start | bytes 2359304 | tf_op jit(solution)/shard_map/ppermute | solution.py:19
  82.2 21.7 %collective-permute-start.10 = (bf16[6,8,8,8,128]{4,3,2,1,0:T(8,128)(2,1)}, bf16[6,8,8,8,128]{4,3,2,1,0:T(8,128)(2,1)S(1)}, u32[]{:S(2)}, u32[]{:S(2)}) collective-permute-start(bf16[6,8,8,8,128]{4,3,2,1,0:T(8,128)(2,1)} %gather_fusion.64), channel_id=1, source_target_pairs={{0,8},{8,16},{16,24},{24,32},{32,40},{40,48},{48,56},{56,64},{64,7... | collective-permute-start | bytes 2359304 | tf_op jit(solution)/shard_map/ppermute | solution.py:19
  86.2 22.1 %collective-permute-start.11 = (bf16[6,8,8,8,128]{4,3,2,1,0:T(8,128)(2,1)}, bf16[6,8,8,8,128]{4,3,2,1,0:T(8,128)(2,1)S(1)}, u32[]{:S(2)}, u32[]{:S(2)}) collective-permute-start(bf16[6,8,8,8,128]{4,3,2,1,0:T(8,128)(2,1)} %gather_fusion.65), channel_id=1, source_target_pairs={{8,0},{16,8},{24,16},{32,24},{40,32},{48,40},{56,48},{64,56},{72,6... | collective-permute-start | bytes 2359304 | tf_op jit(solution)/shard_map/ppermute | solution.py:19
  94.3 10.6 copy-start.2
  113.8 9.1 copy-start.4
  145.2 10.7 copy-start.38
  145.9 10.0 copy-start.40
  155.7 83.8 %copy-start.9 = (bf16[19,8,8,1,128]{4,3,2,1,0:T(2,128)(2,1)S(1)}, bf16[19,8,8,1,128]{4,3,2,1,0:T(2,128)(2,1)}, u32[]{:S(2)}) copy-start(bf16[19,8,8,1,128]{4,3,2,1,0:T(2,128)(2,1)} %get-tuple-element.60) | copy-start | bytes 933892
  282.6 10.2 slice-start.2
  283.4 9.4 slice-start.3
  294.9 27.3 %copy-start.26 = (bf16[27,128,128]{2,1,0:T(8,128)(2,1)S(1)}, bf16[27,128,128]{2,1,0:T(8,128)(2,1)}, u32[]{:S(2)}) copy-start(bf16[27,128,128]{2,1,0:T(8,128)(2,1)} %param.11) | copy-start | bytes 2654212
  297.9 58.6 %copy-start.21 = (bf16[1,8,8,8,128]{4,3,2,1,0:T(8,128)(2,1)S(1)}, bf16[1,8,8,8,128]{4,3,2,1,0:T(8,128)(2,1)}, u32[]{:S(2)}) copy-start(bf16[1,8,8,8,128]{4,3,2,1,0:T(8,128)(2,1)} %copy-done.20) | copy-start | bytes 393220
  300.8 24.1 %collective-permute-start.12 = (bf16[2,8,8,8,128]{4,3,2,1,0:T(8,128)(2,1)}, bf16[2,8,8,8,128]{4,3,2,1,0:T(8,128)(2,1)S(1)}, u32[]{:S(2)}, u32[]{:S(2)}) collective-permute-start(bf16[2,8,8,8,128]{4,3,2,1,0:T(8,128)(2,1)} %gather_fusion.93), channel_id=1, source_target_pairs={{0,1},{1,2},{2,3},{3,4},{4,5},{5,6},{6,7},{8,9},{9,10},{10,11},{11... | collective-permute-start | bytes 786440 | tf_op jit(solution)/shard_map/ppermute | solution.py:19
  307.4 37.7 %collective-permute-start.13 = (bf16[2,8,8,8,128]{4,3,2,1,0:T(8,128)(2,1)}, bf16[2,8,8,8,128]{4,3,2,1,0:T(8,128)(2,1)S(1)}, u32[]{:S(2)}, u32[]{:S(2)}) collective-permute-start(bf16[2,8,8,8,128]{4,3,2,1,0:T(8,128)(2,1)} %gather_fusion.94), channel_id=1, source_target_pairs={{1,0},{2,1},{3,2},{4,3},{5,4},{6,5},{7,6},{9,8},{10,9},{11,10},{12... | collective-permute-start | bytes 786440 | tf_op jit(solution)/shard_map/ppermute | solution.py:19
  311.5 33.7 %collective-permute-start.4 = (bf16[2,8,8,8,128]{4,3,2,1,0:T(8,128)(2,1)}, bf16[2,8,8,8,128]{4,3,2,1,0:T(8,128)(2,1)S(1)}, u32[]{:S(2)}, u32[]{:S(2)}) collective-permute-start(bf16[2,8,8,8,128]{4,3,2,1,0:T(8,128)(2,1)} %gather_fusion.31), channel_id=1, source_target_pairs={{0,1},{1,2},{2,3},{3,4},{4,5},{5,6},{6,7},{8,9},{9,10},{10,11},{11... | collective-permute-start | bytes 786440 | tf_op jit(solution)/shard_map/ppermute | solution.py:19
  317.1 39.3 %collective-permute-start.5 = (bf16[2,8,8,8,128]{4,3,2,1,0:T(8,128)(2,1)}, bf16[2,8,8,8,128]{4,3,2,1,0:T(8,128)(2,1)}, u32[]{:S(2)}, u32[]{:S(2)}) collective-permute-start(bf16[2,8,8,8,128]{4,3,2,1,0:T(8,128)(2,1)} %gather_fusion.32), channel_id=1, source_target_pairs={{1,0},{2,1},{3,2},{4,3},{5,4},{6,5},{7,6},{9,8},{10,9},{11,10},{12... | collective-permute-start | bytes 786440 | tf_op jit(solution)/shard_map/ppermute | solution.py:19
  359.3 25.4 %collective-permute-start.6 = (bf16[6,8,8,8,128]{4,3,2,1,0:T(8,128)(2,1)}, bf16[6,8,8,8,128]{4,3,2,1,0:T(8,128)(2,1)}, u32[]{:S(2)}, u32[]{:S(2)}) collective-permute-start(bf16[6,8,8,8,128]{4,3,2,1,0:T(8,128)(2,1)} %gather_fusion.33), channel_id=1, source_target_pairs={{0,8},{8,16},{16,24},{24,32},{32,40},{40,48},{48,56},{56,64},{64,7... | collective-permute-start | bytes 2359304 | tf_op jit(solution)/shard_map/ppermute | solution.py:19
  370.1 16.7 %collective-permute-start.7 = (bf16[6,8,8,8,128]{4,3,2,1,0:T(8,128)(2,1)}, bf16[6,8,8,8,128]{4,3,2,1,0:T(8,128)(2,1)}, u32[]{:S(2)}, u32[]{:S(2)}) collective-permute-start(bf16[6,8,8,8,128]{4,3,2,1,0:T(8,128)(2,1)} %gather_fusion.34), channel_id=1, source_target_pairs={{8,0},{16,8},{24,16},{32,24},{40,32},{48,40},{56,48},{64,56},{72,6... | collective-permute-start | bytes 2359304 | tf_op jit(solution)/shard_map/ppermute | solution.py:19
  376.3 23.0 %collective-permute-start.14 = (bf16[6,8,8,8,128]{4,3,2,1,0:T(8,128)(2,1)}, bf16[6,8,8,8,128]{4,3,2,1,0:T(8,128)(2,1)S(1)}, u32[]{:S(2)}, u32[]{:S(2)}) collective-permute-start(bf16[6,8,8,8,128]{4,3,2,1,0:T(8,128)(2,1)} %gather_fusion.95), channel_id=1, source_target_pairs={{0,8},{8,16},{16,24},{24,32},{32,40},{40,48},{48,56},{56,64},{64,7... | collective-permute-start | bytes 2359304 | tf_op jit(solution)/shard_map/ppermute | solution.py:19
  379.4 29.3 %collective-permute-start.15 = (bf16[6,8,8,8,128]{4,3,2,1,0:T(8,128)(2,1)}, bf16[6,8,8,8,128]{4,3,2,1,0:T(8,128)(2,1)}, u32[]{:S(2)}, u32[]{:S(2)}) collective-permute-start(bf16[6,8,8,8,128]{4,3,2,1,0:T(8,128)(2,1)} %gather_fusion.96), channel_id=1, source_target_pairs={{8,0},{16,8},{24,16},{32,24},{40,32},{48,40},{56,48},{64,56},{72,6... | collective-permute-start | bytes 2359304 | tf_op jit(solution)/shard_map/ppermute | solution.py:19
  386.8 12.5 %copy-start.3 = (bf16[19,8,8,8,128]{4,3,2,1,0:T(8,128)(2,1)S(1)}, bf16[19,8,8,8,128]{4,3,2,1,0:T(8,128)(2,1)}, u32[]{:S(2)}) copy-start(bf16[19,8,8,8,128]{4,3,2,1,0:T(8,128)(2,1)} %constant_dynamic-update-slice_fusion.102) | copy-start | bytes 7471108
  418.2 41.1 %copy-start.11 = (bf16[19,8,8,1,128]{4,3,2,1,0:T(2,128)(2,1)S(1)}, bf16[19,8,8,1,128]{4,3,2,1,0:T(2,128)(2,1)}, u32[]{:S(2)}) copy-start(bf16[19,8,8,1,128]{4,3,2,1,0:T(2,128)(2,1)} %get-tuple-element.87) | copy-start | bytes 933892
  448.8 12.7 %copy-start.42 = (bf16[2,8,1,1,128]{4,3,2,1,0:T(2,128)(2,1)}, bf16[2,8,1,1,128]{4,3,2,1,0:T(2,128)(2,1)S(1)}, u32[]{:S(2)}) copy-start(bf16[2,8,1,1,128]{4,3,2,1,0:T(2,128)(2,1)S(1)} %copy.211) | copy-start | bytes 12292
  449.5 12.0 %copy-start.44 = (bf16[2,8,1,1,128]{4,3,2,1,0:T(2,128)(2,1)}, bf16[2,8,1,1,128]{4,3,2,1,0:T(2,128)(2,1)S(1)}, u32[]{:S(2)}) copy-start(bf16[2,8,1,1,128]{4,3,2,1,0:T(2,128)(2,1)S(1)} %copy.210) | copy-start | bytes 12292
  457.7 22.4 %copy-start.16 = (bf16[2,8,8,1,128]{4,3,2,1,0:T(2,128)(2,1)}, bf16[2,8,8,1,128]{4,3,2,1,0:T(2,128)(2,1)S(1)}, u32[]{:S(2)}) copy-start(bf16[2,8,8,1,128]{4,3,2,1,0:T(2,128)(2,1)S(1)} %copy.208) | copy-start | bytes 98308
  459.3 23.1 %copy-start.31 = (bf16[2,8,8,128]{3,2,1,0:T(8,128)(2,1)}, bf16[2,8,8,128]{3,2,1,0:T(8,128)(2,1)S(1)}, u32[]{:S(2)}) copy-start(bf16[2,8,8,128]{3,2,1,0:T(8,128)(2,1)S(1)} %gather_fusion.51) | copy-start | bytes 98308
  460.3 33.6 %copy-start.10 = (bf16[19,8,8,1,128]{4,3,2,1,0:T(2,128)(2,1)S(1)}, bf16[19,8,8,1,128]{4,3,2,1,0:T(2,128)(2,1)}, u32[]{:S(2)}) copy-start(bf16[19,8,8,1,128]{4,3,2,1,0:T(2,128)(2,1)} %get-tuple-element.35) | copy-start | bytes 933892
  508.1 7.2 copy-start.32
  508.1 7.2 copy-start.35
  508.1 7.2 copy-start.43
  508.1 7.2 copy-start.45
  508.1 7.2 copy-start.57
  508.2 7.2 copy-start.58
  508.2 7.2 copy-start.61
  508.2 7.2 copy-start.62
  508.2 7.2 copy-start.78
  508.2 7.2 copy-start.79
  508.2 7.2 copy-start.80
  508.2 7.2 copy-start.81
  533.8 594.4 %all-reduce.11.cloned.1.call-start = ((), (), s32[]{:S(2)}) async-start(), calls=%async_computation.1 | async-start | bytes 7077888 | tf_op jit(solution)/shard_map/psum | solution.py:13
  544.9 279.3 %copy-start.53 = (bf16[19,1,1,1,128]{4,3,2,1,0:T(2,128)(2,1)S(1)}, bf16[19,1,1,1,128]{4,3,2,1,0:T(2,128)(2,1)}, u32[]{:S(2)}) copy-start(bf16[19,1,1,1,128]{4,3,2,1,0:T(2,128)(2,1)} %get-tuple-element.10) | copy-start | bytes 14596
  544.9 279.9 %copy-start.52 = (bf16[19,1,1,1,128]{4,3,2,1,0:T(2,128)(2,1)S(1)}, bf16[19,1,1,1,128]{4,3,2,1,0:T(2,128)(2,1)}, u32[]{:S(2)}) copy-start(bf16[19,1,1,1,128]{4,3,2,1,0:T(2,128)(2,1)} %get-tuple-element.11) | copy-start | bytes 14596
  544.9 280.7 %copy-start.51 = (bf16[19,1,1,1,128]{4,3,2,1,0:T(2,128)(2,1)S(1)}, bf16[19,1,1,1,128]{4,3,2,1,0:T(2,128)(2,1)}, u32[]{:S(2)}) copy-start(bf16[19,1,1,1,128]{4,3,2,1,0:T(2,128)(2,1)} %get-tuple-element.12) | copy-start | bytes 14596
  544.9 281.4 %copy-start.50 = (bf16[19,1,1,1,128]{4,3,2,1,0:T(2,128)(2,1)S(1)}, bf16[19,1,1,1,128]{4,3,2,1,0:T(2,128)(2,1)}, u32[]{:S(2)}) copy-start(bf16[19,1,1,1,128]{4,3,2,1,0:T(2,128)(2,1)} %get-tuple-element.13) | copy-start | bytes 14596
  545.7 284.2 %copy-start.34 = (bf16[19,1,8,1,128]{4,3,2,1,0:T(2,128)(2,1)S(1)}, bf16[19,1,8,1,128]{4,3,2,1,0:T(2,128)(2,1)}, u32[]{:S(2)}) copy-start(bf16[19,1,8,1,128]{4,3,2,1,0:T(2,128)(2,1)} %get-tuple-element.22) | copy-start | bytes 116740
  545.7 284.9 %copy-start.33 = (bf16[19,1,8,1,128]{4,3,2,1,0:T(2,128)(2,1)S(1)}, bf16[19,1,8,1,128]{4,3,2,1,0:T(2,128)(2,1)}, u32[]{:S(2)}) copy-start(bf16[19,1,8,1,128]{4,3,2,1,0:T(2,128)(2,1)} %get-tuple-element.23) | copy-start | bytes 116740
  545.7 287.3 %copy-start.23 = (bf16[2,8,1,10,128]{4,3,2,1,0:T(8,128)(2,1)S(1)}, bf16[2,8,1,10,128]{4,3,2,1,0:T(8,128)(2,1)}, u32[]{:S(2)}) copy-start(bf16[2,8,1,10,128]{4,3,2,1,0:T(8,128)(2,1)} %copy-done.22) | copy-start | bytes 122884
  839.8 9.6 slice-start
  840.6 8.8 slice-start.1
  (46 other events, 208.0 us)
Sparse Core Ops, SparseCore 0:
  533.9 289.4 all-reduce.8
  826.3 301.7 all-reduce.10
